TPU v7x, 32 devices: a whole 2x2x4 slice. The times are simulated.
32 devices in a mesh: gx: 8 (over y, x, core), gy: 4 (over z).
Axes of the slice: x: 2, y: 2, z: 4, core: 2. Of those that a mesh axis runs over, the one named last changes fastest.
Arguments:
- previous: float32 [128, 128, 2048], P('gx', 'gy'), may hold values from -1.8 to 1.8
- source: float32 [128, 128, 2048], P('gx', 'gy'), may hold values from -5 to 5
- conductivity: float32 [128, 128, 2048], P('gx', 'gy'), may hold values from 0.24 to 8.1
Outputs:
- correction: float32 [128, 128, 2048], P('gx', 'gy')
All inputs are finite; a program needn't handle non-finite values.
Results may differ from a plain program's by a relative error of at most 0.000068.
Values sent between devices are 32-bit elements; how exact they have to be, the bound alone decides.
A program may use at most 320 MiB of HBM per device.

v0:
```python
import functools

import jax
import jax.numpy as jnp
from jax import lax
from jax.experimental import pallas as pl
from jax.experimental.pallas import tpu as pltpu
from jax.sharding import PartitionSpec as P

F = 16
CSWEEPS = 32
LANES = 128
TOP = 8

reaction = 0.2
damping = 0.8
coarse_factor = 0.25

MESH = pl.DeviceIdType.MESH
HI = lax.Precision.HIGHEST


def lane_index(shape):
    return lax.broadcasted_iota(jnp.int32, shape, len(shape) - 1)


def next_col(here, after):
    first = lane_index(here.shape) == 0
    return pltpu.roll(jnp.where(first, after, here), LANES - 1, 1)


def prev_col(before, here):
    last = lane_index(here.shape) == LANES - 1
    return pltpu.roll(jnp.where(last, before, here), 1, 1)


def main_kernel(
    nx, ny, planes, rows, chunks,
    prev_hbm, src_hbm, cond_hbm, out_hbm, cols_ref,
    cond, prev, corr1, corr2, src, wgt, cx, cy, cz,
    row_send, row_recv, acc, part, gather, coarse,
    load_sem, out_sem, send_sem, recv_sem, psend_sem, precv_sem, gsend_sem, grecv_sem,
):
    gx, gy = lax.axis_index("gx"), lax.axis_index("gy")
    body_rows = pl.ds(TOP, rows)
    up_rows = pl.ds(TOP + 1, rows)
    down_rows = pl.ds(TOP - 1, rows)
    last_row = TOP + rows - 1

    loads = ((cond_hbm, cond, True), (prev_hbm, prev, True), (src_hbm, src, False))
    for k, (hbm, buf, padded) in enumerate(loads):
        for c in range(chunks):
            part_hbm = hbm.at[:, :, pl.ds(c * LANES, LANES)]
            dst = buf.at[pl.ds(1, planes), c, body_rows, :] if padded else buf.at[:, c]
            pltpu.make_async_copy(part_hbm, dst, load_sem.at[k]).start()

    def wait_load(k):
        pltpu.make_async_copy(src, src, load_sem.at[k]).wait()

    barrier = pltpu.get_barrier_semaphore()
    for j in range(1, nx):
        pl.semaphore_signal(barrier, inc=1, device_id=(lax.rem(gx + j, nx), gy), device_id_type=MESH)
    for j in range(1, ny):
        pl.semaphore_signal(barrier, inc=1, device_id=(gx, lax.rem(gy + j, ny)), device_id_type=MESH)
    pl.semaphore_wait(barrier, nx + ny - 2)

    x_next, x_prev = (lax.rem(gx + 1, nx), gy), (lax.rem(gx + nx - 1, nx), gy)
    y_next, y_prev = (gx, lax.rem(gy + 1, ny)), (gx, lax.rem(gy + ny - 1, ny))
    fields = (cond, prev, corr1, corr2)

    def remote(source, target, sem, device):
        return pltpu.make_async_remote_copy(
            src_ref=source, dst_ref=target, send_sem=send_sem.at[sem], recv_sem=recv_sem.at[sem],
            device_id=device, device_id_type=MESH,
        )

    def plane_copies(k):
        buf = fields[k]
        return (
            remote(buf.at[1, :, body_rows, :], buf.at[planes + 1, :, body_rows, :], 4 * k, x_prev),
            remote(buf.at[planes, :, body_rows, :], buf.at[0, :, body_rows, :], 4 * k + 1, x_next),
        )

    def row_copies(k):
        return (
            remote(row_send.at[k, 0], row_recv.at[k, 0], 4 * k + 2, y_prev),
            remote(row_send.at[k, 1], row_recv.at[k, 1], 4 * k + 3, y_next),
        )

    def start_all(copies):
        for copy in copies:
            copy.start()

    def wait_recv(copies):
        for copy in copies:
            copy.wait_recv()

    def pack(k, p, c, block):
        at = (p - 1) * chunks + c
        row_send[k, 0, pl.ds(at, 1), :] = block[0:1]
        row_send[k, 1, pl.ds(at, 1), :] = block[rows - 1 : rows]

    def pack_all(k):
        buf = fields[k]

        @pl.loop(1, planes + 1)
        def _(p):
            for c in range(chunks):
                at = (p - 1) * chunks + c
                row_send[k, 0, pl.ds(at, 1), :] = buf[p, c, TOP : TOP + 1, :]
                row_send[k, 1, pl.ds(at, 1), :] = buf[p, c, last_row : last_row + 1, :]

    def unpack_all(k):
        buf = fields[k]

        @pl.loop(1, planes + 1)
        def _(p):
            for c in range(chunks):
                at = (p - 1) * chunks + c
                buf[p, c, last_row + 1 : last_row + 2, :] = row_recv[k, 0, pl.ds(at, 1), :]
                buf[p, c, TOP - 1 : TOP, :] = row_recv[k, 1, pl.ds(at, 1), :]

    for k in (0, 1):
        wait_load(k)
        start_all(plane_copies(k))
        pack_all(k)
        start_all(row_copies(k))
    acc[...] = jnp.zeros_like(acc)
    wait_load(2)
    for k in (0, 1):
        wait_recv(row_copies(k))
        unpack_all(k)

    half = rows // F

    def add_part(field, c, block):
        for r in range(half):
            piece = block[r * F : r * F + 8] + block[r * F + 8 : r * F + 16]
            at = (field * half + r) * chunks + c
            acc[at] = acc[at] + piece

    def plane_of(i):
        return lax.rem(i + 1, planes) + 1

    @pl.loop(0, planes)
    def _(i):
        p = plane_of(i)

        @pl.when(i == planes - 2)
        def _():
            wait_recv(plane_copies(0))
            wait_recv(plane_copies(1))

        def cond_at(c):
            return cond[p, c % chunks, body_rows, :]

        def prev_at(c):
            return prev[p, c % chunks, body_rows, :]

        k_here = cond_at(chunks - 1)
        k_after = cond_at(0)
        cz_before = k_here + next_col(k_here, k_after)
        q_before = cz_before * prev_at(chunks - 1)
        k_here = k_after
        v_here = prev_at(0)
        for c in range(chunks):
            k_after, v_after = cond_at(c + 1), prev_at(c + 1)
            cz_here = k_here + next_col(k_here, k_after)
            q_here = cz_here * v_here
            cz_low = prev_col(cz_before, cz_here)
            cx_high = k_here + cond[p + 1, c, body_rows, :]
            cx_low = k_here + cond[p - 1, c, body_rows, :]
            cy_high = k_here + cond[p, c, up_rows, :]
            cy_low = k_here + cond[p, c, down_rows, :]
            cz[p - 1, c] = cz_here
            cx[p, c] = cx_high
            cx[p - 1, c] = cx_low
            cy[p - 1, c, body_rows, :] = cy_high
            cy[p - 1, c, TOP - 1 : TOP, :] = cy_low[0:1]
            twice_diag = (((cx_high + cx_low) + (cy_high + cy_low)) + (cz_here + cz_low)) + 2 * reaction
            total = (
                (cx_high * prev[p + 1, c, body_rows, :] + cx_low * prev[p - 1, c, body_rows, :])
                + (cy_high * prev[p, c, up_rows, :] + cy_low * prev[p, c, down_rows, :])
            ) + (cz_here * next_col(v_here, v_after) + prev_col(q_before, q_here))
            resid = src[p - 1, c] - 0.5 * (twice_diag * v_here - total)
            weight = damping / twice_diag
            first = (2.0 * weight) * resid
            wgt[p - 1, c] = weight
            corr1[p, c, body_rows, :] = first
            pack(2, p, c, first)
            add_part(0, c, resid)
            add_part(1, c, k_here)
            k_here, v_here, cz_before, q_before = k_after, v_after, cz_here, q_here

    start_all(plane_copies(2))
    start_all(row_copies(2))

    lines = 2 * half * chunks
    sums = jnp.sum(acc[...], axis=1)
    per_chunk = LANES // F
    lane_row = lax.broadcasted_iota(jnp.int32, (LANES, LANES), 0)
    lane_col = lax.broadcasted_iota(jnp.int32, (LANES, LANES), 1)
    pool = jnp.where(lax.rem(lane_col, per_chunk) == lax.div(lane_row, F), 1.0, 0.0)
    pooled = jnp.dot(sums, pool, precision=HI, preferred_element_type=jnp.float32)
    line_row = lax.broadcasted_iota(jnp.int32, (lines, LANES), 0)
    line_col = lax.broadcasted_iota(jnp.int32, (lines, LANES), 1)
    pooled = jnp.where(lax.div(line_col, per_chunk) == lax.rem(line_row, chunks), pooled, 0.0)
    small = jnp.sum(pooled.reshape(2 * half, chunks, LANES), axis=1) * (1.0 / (F * F * F))
    part[gy, 0 : 2 * half, :] = small

    def part_copy(j):
        return pltpu.make_async_remote_copy(
            src_ref=part.at[gy], dst_ref=part.at[gy], send_sem=psend_sem.at[j], recv_sem=precv_sem.at[j],
            device_id=(gx, lax.rem(gy + j, ny)), device_id_type=MESH,
        )

    def part_arrival(j):
        at = lax.rem(gy + ny - j, ny)
        return pltpu.make_async_remote_copy(
            src_ref=part.at[at], dst_ref=part.at[at], send_sem=psend_sem.at[j], recv_sem=precv_sem.at[j],
            device_id=(gx, lax.rem(gy + j, ny)), device_id_type=MESH,
        )

    def gather_copy(j):
        return pltpu.make_async_remote_copy(
            src_ref=gather.at[gx], dst_ref=gather.at[gx], send_sem=gsend_sem.at[j], recv_sem=grecv_sem.at[j],
            device_id=(lax.rem(gx + j, nx), gy), device_id_type=MESH,
        )

    def gather_arrival(j):
        at = lax.rem(gx + nx - j, nx)
        return pltpu.make_async_remote_copy(
            src_ref=gather.at[at], dst_ref=gather.at[at], send_sem=gsend_sem.at[j], recv_sem=grecv_sem.at[j],
            device_id=(lax.rem(gx + j, nx), gy), device_id_type=MESH,
        )

    for j in range(1, ny):
        part_copy(j).start()

    wait_recv(row_copies(2))
    unpack_all(2)

    for j in range(1, ny):
        part_arrival(j).wait_recv()
    for y in range(ny):
        for f in range(2):
            gather[gx, f, y * half : (y + 1) * half, :] = part[y, f * half : (f + 1) * half, :]
    for j in range(1, nx):
        gather_copy(j).start()

    def sweep(k, buf, write):
        @pl.loop(0, planes)
        def _(i):
            p = plane_of(i)

            @pl.when(i == planes - 2)
            def _():
                wait_recv(plane_copies(k))

            def at(c):
                return buf[p, c % chunks, body_rows, :]

            q_before = cz[p - 1, chunks - 1] * at(chunks - 1)
            here = at(0)
            for c in range(chunks):
                after = at(c + 1)
                cz_here = cz[p - 1, c]
                q_here = cz_here * here
                total = (
                    (cx[p, c] * buf[p + 1, c, body_rows, :] + cx[p - 1, c] * buf[p - 1, c, body_rows, :])
                    + (
                        cy[p - 1, c, body_rows, :] * buf[p, c, up_rows, :]
                        + cy[p - 1, c, down_rows, :] * buf[p, c, down_rows, :]
                    )
                ) + (cz_here * next_col(here, after) + prev_col(q_before, q_here))
                write(p, c, here, wgt[p - 1, c] * total)
                here, q_before = after, q_here

            if k == 3:
                @pl.when((lax.rem(i, 4) == 3) & (i < planes - 1))
                def _():
                    store_planes(i - 2, 4)

    def write_second(p, c, here, term):
        second = (1.0 + (1.0 - damping)) * here + term
        corr2[p, c, body_rows, :] = second
        pack(3, p, c, second)

    sweep(2, corr1, write_second)
    start_all(plane_copies(3))
    start_all(row_copies(3))

    for j in range(1, nx):
        gather_arrival(j).wait_recv()
    crows = ny * half
    resid = gather[:, 0]
    ccond = gather[:, 1]

    def around(v):
        return (
            jnp.concatenate([v[1:], v[:1]], axis=0), jnp.concatenate([v[-1:], v[:-1]], axis=0),
            pltpu.roll(v, crows - 1, 1), pltpu.roll(v, 1, 1),
            pltpu.roll(v, 1, 2), pltpu.roll(v, LANES - 1, 2),
        )

    ccoup = [(0.5 * coarse_factor) * (ccond + near) for near in around(ccond)]
    cdiag = jnp.full_like(ccond, reaction)
    for one in ccoup:
        cdiag = cdiag + one
    cwgt = damping / cdiag
    ccoup = [cwgt * one for one in ccoup]
    cfirst = cwgt * resid

    def coarse_step(_, v):
        result = (1.0 - damping) * v + cfirst
        for one, near in zip(ccoup, around(v)):
            result = result + one * near
        return result

    coarse[...] = lax.fori_loop(0, CSWEEPS - 1, coarse_step, cfirst)
    turn = lax.rem(2 * crows + 1 - gy * half, crows)
    block = []
    for a in range(3):
        plane = coarse[lax.rem(gx + nx - 1 + a, nx)]
        block.append(pltpu.roll(plane, turn, 0)[0:8])
    block = jnp.concatenate(block, axis=0)
    ccols = chunks * LANES // F
    for c in range(chunks):
        fine = c * LANES + lane_col
        base = lax.div(fine, F)
        offset = (lax.rem(fine, F).astype(jnp.float32) + 0.5) / F - 0.5
        side = lax.rem(jnp.where(offset > 0, base + 1, base + ccols - 1), ccols)
        spread = jnp.where(lane_row == base, 1.0 - jnp.abs(offset), 0.0)
        spread = spread + jnp.where(lane_row == side, jnp.abs(offset), 0.0)
        cols_ref[:, c * LANES : (c + 1) * LANES] = jnp.dot(
            block, spread, precision=HI, preferred_element_type=jnp.float32
        )

    wait_recv(row_copies(3))
    unpack_all(3)

    def out_copy(c, start, count):
        return pltpu.make_async_copy(
            src.at[pl.ds(start, count), c],
            out_hbm.at[pl.ds(start, count), :, pl.ds(c * LANES, LANES)],
            out_sem,
        )

    def store_planes(start, count):
        for c in range(chunks):
            out_copy(c, start, count).start()

    def write_third(p, c, here, term):
        src[p - 1, c] = ((1.0 - damping) * here + corr1[p, c, body_rows, :]) + term

    sweep(3, corr2, write_third)
    store_planes(planes - 3, 3)
    store_planes(0, 1)

    for k in range(4):
        for copy in plane_copies(k) + row_copies(k):
            copy.wait_send()
    for j in range(1, ny):
        part_copy(j).wait_send()
    for j in range(1, nx):
        gather_copy(j).wait_send()
    pltpu.make_async_copy(src, src, out_sem).wait()


def add_kernel(step_planes, rows, fine_ref, cols_ref, out_ref, across):
    step = pl.program_id(0)
    half = rows // F

    @pl.when(step == 0)
    def _():
        row = lax.broadcasted_iota(jnp.int32, (rows, LANES), 0)
        base = lax.div(row, F) + 1
        offset = (lax.rem(row, F).astype(jnp.float32) + 0.5) / F - 0.5
        side = jnp.where(offset > 0, base + 1, base - 1)
        weights = [
            jnp.where(base == b, 1.0 - jnp.abs(offset), 0.0) + jnp.where(side == b, jnp.abs(offset), 0.0)
            for b in range(half + 2)
        ]
        for a in range(3):
            for c in range(cols_ref.shape[1] // LANES):
                at = pl.ds(c * LANES, LANES)
                total = weights[0] * cols_ref[8 * a : 8 * a + 1, at]
                for b in range(1, half + 2):
                    total = total + weights[b] * cols_ref[8 * a + b : 8 * a + b + 1, at]
                across[a, :, at] = total

    for q in range(step_planes):
        plane = step * step_planes + q
        offset = (plane.astype(jnp.float32) + 0.5) / F - 0.5
        side = jnp.where(offset > 0, 2, 0)
        weight = jnp.abs(offset)
        out_ref[q] = fine_ref[q] + ((1.0 - weight) * across[1] + weight * across[side])


def per_device(nx, ny, previous, source, conductivity):
    planes, rows, cols = previous.shape
    chunks = cols // LANES
    half = rows // F
    f32 = jnp.float32
    padded = pltpu.VMEM((planes + 2, chunks, rows + 16, LANES), f32)
    plain = pltpu.VMEM((planes, chunks, rows, LANES), f32)
    any_spec = pl.BlockSpec(memory_space=pl.ANY)
    fine, along = pl.pallas_call(
        functools.partial(main_kernel, nx, ny, planes, rows, chunks),
        out_shape=(
            jax.ShapeDtypeStruct((planes, rows, cols), f32),
            jax.ShapeDtypeStruct((24, cols), f32),
        ),
        in_specs=[any_spec] * 3,
        out_specs=(any_spec, pl.BlockSpec(memory_space=pltpu.VMEM)),
        scratch_shapes=[
            padded, padded, padded, padded, plain, plain,
            pltpu.VMEM((planes + 1, chunks, rows, LANES), f32),
            pltpu.VMEM((planes, chunks, rows + 8, LANES), f32),
            plain,
            pltpu.VMEM((4, 2, planes * chunks, LANES), f32),
            pltpu.VMEM((4, 2, planes * chunks, LANES), f32),
            pltpu.VMEM((2 * half * chunks, 8, LANES), f32),
            pltpu.VMEM((ny, 8, LANES), f32),
            pltpu.VMEM((nx, 2, ny * half, LANES), f32),
            pltpu.VMEM((nx, ny * half, LANES), f32),
            pltpu.SemaphoreType.DMA((3,)),
            pltpu.SemaphoreType.DMA,
            pltpu.SemaphoreType.DMA((16,)),
            pltpu.SemaphoreType.DMA((16,)),
            pltpu.SemaphoreType.DMA((ny,)),
            pltpu.SemaphoreType.DMA((ny,)),
            pltpu.SemaphoreType.DMA((nx,)),
            pltpu.SemaphoreType.DMA((nx,)),
        ],
        compiler_params=pltpu.CompilerParams(
            collective_id=0, has_side_effects=True, vmem_limit_bytes=60 * 1024 * 1024
        ),
        name="correction_main",
    )(previous, source, conductivity)
    step_planes = 4
    return pl.pallas_call(
        functools.partial(add_kernel, step_planes, rows),
        out_shape=jax.ShapeDtypeStruct((planes, rows, cols), f32),
        grid=(planes // step_planes,),
        in_specs=[
            pl.BlockSpec((step_planes, rows, cols), lambda i: (i, 0, 0)),
            pl.BlockSpec((24, cols), lambda i: (0, 0)),
        ],
        out_specs=pl.BlockSpec((step_planes, rows, cols), lambda i: (i, 0, 0)),
        scratch_shapes=[pltpu.VMEM((3, rows, cols), f32)],
        compiler_params=pltpu.CompilerParams(vmem_limit_bytes=32 * 1024 * 1024),
        name="interpolate_add",
    )(fine, along)


def solution(mesh):
    placed = P("gx", "gy", None)
    nx, ny = mesh.shape["gx"], mesh.shape["gy"]
    return jax.shard_map(
        functools.partial(per_device, nx, ny), mesh=mesh, in_specs=(placed,) * 3, out_specs=placed,
        check_vma=False,
    )
```

profile of v0, /device:TPU:0, one launch (start us, length us, event | category | flops | bytes accessed | tf_op | source)
XLA Modules:
  0.0 65.6 jit_solution(10285383632697757027)
XLA Ops:
  0.0 59.7 %correction_main.1 = (f32[16,32,2048]{2,1,0:T(8,128)}, f32[24,2048]{1,0:T(8,128)}) custom-call(f32[16,32,2048]{2,1,0:T(8,128)} %prev_hbm.1, f32[16,32,2048]{2,1,0:T(8,128)} %src_hbm.1, f32[16,32,2048]{2,1,0:T(8,128)} %cond_hbm.1), custom_call_target="tpu_custom_call" | custom-call | tf_op jit(solution)/shard_map/correction_main/pallas_call | solution.py:408
  59.7 0.0 copy-start
  59.7 2.2 %copy-done = f32[16,32,2048]{2,1,0:T(8,128)S(1)} copy-done((f32[16,32,2048]{2,1,0:T(8,128)S(1)}, f32[16,32,2048]{2,1,0:T(8,128)}, u32[]{:S(2)}) %copy-start) | copy-done | bytes 4194328
  61.9 0.0 copy-start.1
  61.9 0.9 %copy-done.1 = f32[24,2048]{1,0:T(8,128)S(1)} copy-done((f32[24,2048]{1,0:T(8,128)S(1)}, f32[24,2048]{1,0:T(8,128)}, u32[]{:S(2)}) %copy-start.1) | copy-done | bytes 196632
  62.8 2.8 %interpolate_add.1 = f32[16,32,2048]{2,1,0:T(8,128)} custom-call(f32[16,32,2048]{2,1,0:T(8,128)S(1)} %copy-done, f32[24,2048]{1,0:T(8,128)S(1)} %copy-done.1), custom_call_target="tpu_custom_call" | custom-call | tf_op jit(solution)/shard_map/interpolate_add/pallas_call | solution.py:442
Async XLA Ops:
  59.7 2.2 %copy-start = (f32[16,32,2048]{2,1,0:T(8,128)S(1)}, f32[16,32,2048]{2,1,0:T(8,128)}, u32[]{:S(2)}) copy-start(f32[16,32,2048]{2,1,0:T(8,128)} %get-tuple-element.7.fine_ref) | copy-start | bytes 12582916
  61.9 0.9 %copy-start.1 = (f32[24,2048]{1,0:T(8,128)S(1)}, f32[24,2048]{1,0:T(8,128)}, u32[]{:S(2)}) copy-start(f32[24,2048]{1,0:T(8,128)} %get-tuple-element.8.cols_ref) | copy-start | bytes 589828
where the time goes:
time: 65.8 us; the launch traced here: 65.6 us
  Pallas kernels  62.5 us (95%)
  local copies, waits for them, and re-layouts  3.11 us (5%)
    pallas_call x1, Pallas kernels, per_device(): pl.pallas_call(functools.partial(main_kernel, nx, ny, planes, rows, chunk...  59.7 us
    unnamed x4, local copies, waits for them, and re-layouts  3.11 us
    pallas_call x1, Pallas kernels, per_device(): pl.pallas_call(functools.partial(add_kernel, step_planes, rows), out_shap...  2.77 us

commit v1 on v0

--- a/solution.py
+++ b/solution.py
@@ -43,9 +43,28 @@
 ):
     gx, gy = lax.axis_index("gx"), lax.axis_index("gy")
     body_rows = pl.ds(TOP, rows)
-    up_rows = pl.ds(TOP + 1, rows)
-    down_rows = pl.ds(TOP - 1, rows)
     last_row = TOP + rows - 1
+    inner = planes - 2
+    steps = 2 * planes
+
+    def place_of(i):
+        late = lax.div(i, 2 * inner)
+        past = i - 2 * inner
+        edge = (1 - late) * lax.div(i, inner) + late * lax.rem(past, 2)
+        order = (1 - late) * lax.rem(i, inner) + late * (inner + lax.div(past, 2))
+        return lax.rem(order + 1, planes) + 1, order, edge
+
+    def tiles(edge):
+        low = TOP + rows // 2 - 8 - (rows // 2 - 8) * edge
+        high = TOP + rows // 2 + (rows // 2 - 8) * edge
+        return pl.multiple_of(low, 8), pl.multiple_of(high, 8)
+
+    def get(ref, p, c, at, shift=0):
+        return jnp.concatenate([ref[p, c, pl.ds(t + shift, 8), :] for t in at], axis=0)
+
+    def put(ref, p, c, at, block):
+        ref[p, c, pl.ds(at[0], 8), :] = block[0:8]
+        ref[p, c, pl.ds(at[1], 8), :] = block[8:16]
 
     loads = ((cond_hbm, cond, True), (prev_hbm, prev, True), (src_hbm, src, False))
     for k, (hbm, buf, padded) in enumerate(loads):
@@ -77,14 +96,18 @@
     def plane_copies(k):
         buf = fields[k]
         return (
-            remote(buf.at[1, :, body_rows, :], buf.at[planes + 1, :, body_rows, :], 4 * k, x_prev),
-            remote(buf.at[planes, :, body_rows, :], buf.at[0, :, body_rows, :], 4 * k + 1, x_next),
-        )
-
-    def row_copies(k):
+            remote(buf.at[1, :, body_rows, :], buf.at[planes + 1, :, body_rows, :], 2 * k, x_prev),
+            remote(buf.at[planes, :, body_rows, :], buf.at[0, :, body_rows, :], 2 * k + 1, x_next),
+        )
+
+    cut = inner * chunks
+
+    def row_copies(k, late):
+        lines = pl.ds(cut, 2 * chunks) if late else pl.ds(0, cut)
+        sem = 16 + 4 * k + 2 * late
         return (
-            remote(row_send.at[k, 0], row_recv.at[k, 0], 4 * k + 2, y_prev),
-            remote(row_send.at[k, 1], row_recv.at[k, 1], 4 * k + 3, y_next),
+            remote(row_send.at[k, 0, lines], row_recv.at[k, 0, lines], sem, y_prev),
+            remote(row_send.at[k, 1, lines], row_recv.at[k, 1, lines], sem + 1, y_next),
         )
 
     def start_all(copies):
@@ -95,67 +118,77 @@
         for copy in copies:
             copy.wait_recv()
 
-    def pack(k, p, c, block):
-        at = (p - 1) * chunks + c
+    def pack(k, order, c, block):
+        at = order * chunks + c
         row_send[k, 0, pl.ds(at, 1), :] = block[0:1]
-        row_send[k, 1, pl.ds(at, 1), :] = block[rows - 1 : rows]
+        row_send[k, 1, pl.ds(at, 1), :] = block[15:16]
 
     def pack_all(k):
         buf = fields[k]
 
-        @pl.loop(1, planes + 1)
-        def _(p):
+        @pl.loop(0, planes)
+        def _(order):
+            p = lax.rem(order + 1, planes) + 1
             for c in range(chunks):
-                at = (p - 1) * chunks + c
+                at = order * chunks + c
                 row_send[k, 0, pl.ds(at, 1), :] = buf[p, c, TOP : TOP + 1, :]
                 row_send[k, 1, pl.ds(at, 1), :] = buf[p, c, last_row : last_row + 1, :]
 
-    def unpack_all(k):
+    def unpack(k, first, last):
         buf = fields[k]
 
-        @pl.loop(1, planes + 1)
-        def _(p):
+        @pl.loop(first, last)
+        def _(order):
+            p = lax.rem(order + 1, planes) + 1
             for c in range(chunks):
-                at = (p - 1) * chunks + c
+                at = order * chunks + c
                 buf[p, c, last_row + 1 : last_row + 2, :] = row_recv[k, 0, pl.ds(at, 1), :]
                 buf[p, c, TOP - 1 : TOP, :] = row_recv[k, 1, pl.ds(at, 1), :]
+
+    def arrivals(i, ks, sent=None):
+        @pl.when(i == inner)
+        def _():
+            for k in ks:
+                wait_recv(row_copies(k, 0))
+                unpack(k, 0, inner)
+
+        @pl.when(i == 2 * inner)
+        def _():
+            if sent is not None:
+                start_all(row_copies(sent, 0))
+            for k in ks:
+                wait_recv(row_copies(k, 1))
+                unpack(k, inner, planes)
+                wait_recv(plane_copies(k))
 
     for k in (0, 1):
         wait_load(k)
         start_all(plane_copies(k))
         pack_all(k)
-        start_all(row_copies(k))
+        start_all(row_copies(k, 0))
+        start_all(row_copies(k, 1))
     acc[...] = jnp.zeros_like(acc)
     wait_load(2)
-    for k in (0, 1):
-        wait_recv(row_copies(k))
-        unpack_all(k)
 
     half = rows // F
 
     def add_part(field, c, block):
         for r in range(half):
-            piece = block[r * F : r * F + 8] + block[r * F + 8 : r * F + 16]
             at = (field * half + r) * chunks + c
-            acc[at] = acc[at] + piece
-
-    def plane_of(i):
-        return lax.rem(i + 1, planes) + 1
-
-    @pl.loop(0, planes)
+            acc[at] = acc[at] + block[8 * r : 8 * r + 8]
+
+    @pl.loop(0, steps)
     def _(i):
-        p = plane_of(i)
-
-        @pl.when(i == planes - 2)
-        def _():
-            wait_recv(plane_copies(0))
-            wait_recv(plane_copies(1))
+        p, order, edge = place_of(i)
+        at = tiles(edge)
+        flat = tuple(pl.multiple_of(t - TOP, 8) for t in at)
+        arrivals(i, (0, 1), 2)
 
         def cond_at(c):
-            return cond[p, c % chunks, body_rows, :]
+            return get(cond, p, c % chunks, at)
 
         def prev_at(c):
-            return prev[p, c % chunks, body_rows, :]
+            return get(prev, p, c % chunks, at)
 
         k_here = cond_at(chunks - 1)
         k_after = cond_at(0)
@@ -168,32 +201,32 @@
             cz_here = k_here + next_col(k_here, k_after)
             q_here = cz_here * v_here
             cz_low = prev_col(cz_before, cz_here)
-            cx_high = k_here + cond[p + 1, c, body_rows, :]
-            cx_low = k_here + cond[p - 1, c, body_rows, :]
-            cy_high = k_here + cond[p, c, up_rows, :]
-            cy_low = k_here + cond[p, c, down_rows, :]
-            cz[p - 1, c] = cz_here
-            cx[p, c] = cx_high
-            cx[p - 1, c] = cx_low
-            cy[p - 1, c, body_rows, :] = cy_high
-            cy[p - 1, c, TOP - 1 : TOP, :] = cy_low[0:1]
+            cx_high = k_here + get(cond, p + 1, c, at)
+            cx_low = k_here + get(cond, p - 1, c, at)
+            cy_high = k_here + get(cond, p, c, at, 1)
+            cy_low = k_here + get(cond, p, c, at, -1)
+            put(cz, p - 1, c, flat, cz_here)
+            put(cx, p, c, flat, cx_high)
+            put(cx, p - 1, c, flat, cx_low)
+            put(cy, p - 1, c, at, cy_high)
+            cy[p - 1, c, pl.ds(at[0] - 1, 1), :] = cy_low[0:1]
             twice_diag = (((cx_high + cx_low) + (cy_high + cy_low)) + (cz_here + cz_low)) + 2 * reaction
             total = (
-                (cx_high * prev[p + 1, c, body_rows, :] + cx_low * prev[p - 1, c, body_rows, :])
-                + (cy_high * prev[p, c, up_rows, :] + cy_low * prev[p, c, down_rows, :])
+                (cx_high * get(prev, p + 1, c, at) + cx_low * get(prev, p - 1, c, at))
+                + (cy_high * get(prev, p, c, at, 1) + cy_low * get(prev, p, c, at, -1))
             ) + (cz_here * next_col(v_here, v_after) + prev_col(q_before, q_here))
-            resid = src[p - 1, c] - 0.5 * (twice_diag * v_here - total)
+            resid = get(src, p - 1, c, flat) - 0.5 * (twice_diag * v_here - total)
             weight = damping / twice_diag
             first = (2.0 * weight) * resid
-            wgt[p - 1, c] = weight
-            corr1[p, c, body_rows, :] = first
-            pack(2, p, c, first)
+            put(wgt, p - 1, c, flat, weight)
+            put(corr1, p, c, at, first)
+            pack(2, order, c, first)
             add_part(0, c, resid)
             add_part(1, c, k_here)
             k_here, v_here, cz_before, q_before = k_after, v_after, cz_here, q_here
 
     start_all(plane_copies(2))
-    start_all(row_copies(2))
+    start_all(row_copies(2, 1))
 
     lines = 2 * half * chunks
     sums = jnp.sum(acc[...], axis=1)
@@ -237,58 +270,57 @@
     for j in range(1, ny):
         part_copy(j).start()
 
-    wait_recv(row_copies(2))
-    unpack_all(2)
-
-    for j in range(1, ny):
-        part_arrival(j).wait_recv()
-    for y in range(ny):
-        for f in range(2):
-            gather[gx, f, y * half : (y + 1) * half, :] = part[y, f * half : (f + 1) * half, :]
-    for j in range(1, nx):
-        gather_copy(j).start()
-
-    def sweep(k, buf, write):
-        @pl.loop(0, planes)
+    def pass_on():
+        for j in range(1, ny):
+            part_arrival(j).wait_recv()
+        for y in range(ny):
+            for f in range(2):
+                gather[gx, f, y * half : (y + 1) * half, :] = part[y, f * half : (f + 1) * half, :]
+        for j in range(1, nx):
+            gather_copy(j).start()
+
+    def sweep(k, buf, write, sent=None):
+        @pl.loop(0, steps)
         def _(i):
-            p = plane_of(i)
-
-            @pl.when(i == planes - 2)
-            def _():
-                wait_recv(plane_copies(k))
-
-            def at(c):
-                return buf[p, c % chunks, body_rows, :]
-
-            q_before = cz[p - 1, chunks - 1] * at(chunks - 1)
-            here = at(0)
+            p, order, edge = place_of(i)
+            at = tiles(edge)
+            flat = tuple(pl.multiple_of(t - TOP, 8) for t in at)
+            if k == 2:
+                pl.when(i == inner // 2)(pass_on)
+            arrivals(i, (k,), sent)
+
+            def here_at(c):
+                return get(buf, p, c % chunks, at)
+
+            q_before = get(cz, p - 1, chunks - 1, flat) * here_at(chunks - 1)
+            here = here_at(0)
             for c in range(chunks):
-                after = at(c + 1)
-                cz_here = cz[p - 1, c]
+                after = here_at(c + 1)
+                cz_here = get(cz, p - 1, c, flat)
                 q_here = cz_here * here
                 total = (
-                    (cx[p, c] * buf[p + 1, c, body_rows, :] + cx[p - 1, c] * buf[p - 1, c, body_rows, :])
+                    (get(cx, p, c, flat) * get(buf, p + 1, c, at) + get(cx, p - 1, c, flat) * get(buf, p - 1, c, at))
                     + (
-                        cy[p - 1, c, body_rows, :] * buf[p, c, up_rows, :]
-                        + cy[p - 1, c, down_rows, :] * buf[p, c, down_rows, :]
+                        get(cy, p - 1, c, at) * get(buf, p, c, at, 1)
+                        + get(cy, p - 1, c, at, -1) * get(buf, p, c, at, -1)
                     )
                 ) + (cz_here * next_col(here, after) + prev_col(q_before, q_here))
-                write(p, c, here, wgt[p - 1, c] * total)
+                write(p, order, c, at, flat, here, get(wgt, p - 1, c, flat) * total)
                 here, q_before = after, q_here
 
             if k == 3:
-                @pl.when((lax.rem(i, 4) == 3) & (i < planes - 1))
+                @pl.when((i >= inner) & (i < 2 * inner) & (lax.rem(i - inner, 4) == 3))
                 def _():
-                    store_planes(i - 2, 4)
-
-    def write_second(p, c, here, term):
+                    store_planes(i - inner - 2, 4)
+
+    def write_second(p, order, c, at, flat, here, term):
         second = (1.0 + (1.0 - damping)) * here + term
-        corr2[p, c, body_rows, :] = second
-        pack(3, p, c, second)
-
-    sweep(2, corr1, write_second)
+        put(corr2, p, c, at, second)
+        pack(3, order, c, second)
+
+    sweep(2, corr1, write_second, 3)
     start_all(plane_copies(3))
-    start_all(row_copies(3))
+    start_all(row_copies(3, 1))
 
     for j in range(1, nx):
         gather_arrival(j).wait_recv()
@@ -336,9 +368,6 @@
             block, spread, precision=HI, preferred_element_type=jnp.float32
         )
 
-    wait_recv(row_copies(3))
-    unpack_all(3)
-
     def out_copy(c, start, count):
         return pltpu.make_async_copy(
             src.at[pl.ds(start, count), c],
@@ -350,15 +379,15 @@
         for c in range(chunks):
             out_copy(c, start, count).start()
 
-    def write_third(p, c, here, term):
-        src[p - 1, c] = ((1.0 - damping) * here + corr1[p, c, body_rows, :]) + term
+    def write_third(p, order, c, at, flat, here, term):
+        put(src, p - 1, c, flat, ((1.0 - damping) * here + get(corr1, p, c, at)) + term)
 
     sweep(3, corr2, write_third)
     store_planes(planes - 3, 3)
     store_planes(0, 1)
 
     for k in range(4):
-        for copy in plane_copies(k) + row_copies(k):
+        for copy in plane_copies(k) + row_copies(k, 0) + row_copies(k, 1):
             copy.wait_send()
     for j in range(1, ny):
         part_copy(j).wait_send()
@@ -426,8 +455,8 @@
             pltpu.VMEM((nx, ny * half, LANES), f32),
             pltpu.SemaphoreType.DMA((3,)),
             pltpu.SemaphoreType.DMA,
-            pltpu.SemaphoreType.DMA((16,)),
-            pltpu.SemaphoreType.DMA((16,)),
+            pltpu.SemaphoreType.DMA((32,)),
+            pltpu.SemaphoreType.DMA((32,)),
             pltpu.SemaphoreType.DMA((ny,)),
             pltpu.SemaphoreType.DMA((ny,)),
             pltpu.SemaphoreType.DMA((nx,)),
@@ -449,7 +478,7 @@
         ],
         out_specs=pl.BlockSpec((step_planes, rows, cols), lambda i: (i, 0, 0)),
         scratch_shapes=[pltpu.VMEM((3, rows, cols), f32)],
-        compiler_params=pltpu.CompilerParams(vmem_limit_bytes=32 * 1024 * 1024),
+        compiler_params=pltpu.CompilerParams(vmem_limit_bytes=60 * 1024 * 1024),
         name="interpolate_add",
     )(fine, along)
 

time: 65.8 us -> 55.5 us (0.84)
  Pallas kernels: 62.5 us -> 55.2 us
  local copies, waits for them, and re-layouts: 3.11 us -> 0 us
    pallas_call x1, Pallas kernels: 59.7 us -> 50.2 us  [per_device(): pl.pallas_call(functools.partial(main_kernel, nx, ny, planes, rows, chunk...]
    unnamed x4 -> x0, local copies, waits for them, and re-layouts: 3.11 us -> none
    pallas_call x1, Pallas kernels: 2.77 us -> 5.07 us  [per_device(): pl.pallas_call(functools.partial(add_kernel, step_planes, rows), out_shap...]
where the time goes in v1:
time: 55.5 us; the launch traced here: 55.3 us
  Pallas kernels  55.2 us (99%)
    pallas_call x1, Pallas kernels, per_device(): pl.pallas_call(functools.partial(main_kernel, nx, ny, planes, rows, chunk...  50.2 us
    pallas_call x1, Pallas kernels, per_device(): pl.pallas_call(functools.partial(add_kernel, step_planes, rows), out_shap...  5.07 us

profile of v1, /device:TPU:0, one launch (start us, length us, event | category | flops | bytes accessed | tf_op | source)
XLA Modules:
  0.0 55.3 jit_solution(12555718549446599267)
XLA Ops:
  0.0 50.2 %correction_main.1 = (f32[16,32,2048]{2,1,0:T(8,128)}, f32[24,2048]{1,0:T(8,128)}) custom-call(f32[16,32,2048]{2,1,0:T(8,128)} %prev_hbm.1, f32[16,32,2048]{2,1,0:T(8,128)} %src_hbm.1, f32[16,32,2048]{2,1,0:T(8,128)} %cond_hbm.1), custom_call_target="tpu_custom_call" | custom-call | tf_op jit(solution)/shard_map/correction_main/pallas_call | solution.py:437
  50.2 5.1 %interpolate_add.1 = f32[16,32,2048]{2,1,0:T(8,128)} custom-call(f32[16,32,2048]{2,1,0:T(8,128)} %get-tuple-element.7.fine_ref, f32[24,2048]{1,0:T(8,128)} %get-tuple-element.8.cols_ref), custom_call_target="tpu_custom_call" | custom-call | tf_op jit(solution)/shard_map/interpolate_add/pallas_call | solution.py:471

commit v2 on v1

--- a/solution.py
+++ b/solution.py
@@ -168,7 +168,6 @@
         start_all(row_copies(k, 0))
         start_all(row_copies(k, 1))
     acc[...] = jnp.zeros_like(acc)
-    wait_load(2)
 
     half = rows // F
 
@@ -182,24 +181,18 @@
         p, order, edge = place_of(i)
         at = tiles(edge)
         flat = tuple(pl.multiple_of(t - TOP, 8) for t in at)
-        arrivals(i, (0, 1), 2)
+        arrivals(i, (0,))
 
         def cond_at(c):
             return get(cond, p, c % chunks, at)
-
-        def prev_at(c):
-            return get(prev, p, c % chunks, at)
 
         k_here = cond_at(chunks - 1)
         k_after = cond_at(0)
         cz_before = k_here + next_col(k_here, k_after)
-        q_before = cz_before * prev_at(chunks - 1)
         k_here = k_after
-        v_here = prev_at(0)
         for c in range(chunks):
-            k_after, v_after = cond_at(c + 1), prev_at(c + 1)
+            k_after = cond_at(c + 1)
             cz_here = k_here + next_col(k_here, k_after)
-            q_here = cz_here * v_here
             cz_low = prev_col(cz_before, cz_here)
             cx_high = k_here + get(cond, p + 1, c, at)
             cx_low = k_here + get(cond, p - 1, c, at)
@@ -211,73 +204,9 @@
             put(cy, p - 1, c, at, cy_high)
             cy[p - 1, c, pl.ds(at[0] - 1, 1), :] = cy_low[0:1]
             twice_diag = (((cx_high + cx_low) + (cy_high + cy_low)) + (cz_here + cz_low)) + 2 * reaction
-            total = (
-                (cx_high * get(prev, p + 1, c, at) + cx_low * get(prev, p - 1, c, at))
-                + (cy_high * get(prev, p, c, at, 1) + cy_low * get(prev, p, c, at, -1))
-            ) + (cz_here * next_col(v_here, v_after) + prev_col(q_before, q_here))
-            resid = get(src, p - 1, c, flat) - 0.5 * (twice_diag * v_here - total)
-            weight = damping / twice_diag
-            first = (2.0 * weight) * resid
-            put(wgt, p - 1, c, flat, weight)
-            put(corr1, p, c, at, first)
-            pack(2, order, c, first)
-            add_part(0, c, resid)
+            put(wgt, p - 1, c, flat, twice_diag)
             add_part(1, c, k_here)
-            k_here, v_here, cz_before, q_before = k_after, v_after, cz_here, q_here
-
-    start_all(plane_copies(2))
-    start_all(row_copies(2, 1))
-
-    lines = 2 * half * chunks
-    sums = jnp.sum(acc[...], axis=1)
-    per_chunk = LANES // F
-    lane_row = lax.broadcasted_iota(jnp.int32, (LANES, LANES), 0)
-    lane_col = lax.broadcasted_iota(jnp.int32, (LANES, LANES), 1)
-    pool = jnp.where(lax.rem(lane_col, per_chunk) == lax.div(lane_row, F), 1.0, 0.0)
-    pooled = jnp.dot(sums, pool, precision=HI, preferred_element_type=jnp.float32)
-    line_row = lax.broadcasted_iota(jnp.int32, (lines, LANES), 0)
-    line_col = lax.broadcasted_iota(jnp.int32, (lines, LANES), 1)
-    pooled = jnp.where(lax.div(line_col, per_chunk) == lax.rem(line_row, chunks), pooled, 0.0)
-    small = jnp.sum(pooled.reshape(2 * half, chunks, LANES), axis=1) * (1.0 / (F * F * F))
-    part[gy, 0 : 2 * half, :] = small
-
-    def part_copy(j):
-        return pltpu.make_async_remote_copy(
-            src_ref=part.at[gy], dst_ref=part.at[gy], send_sem=psend_sem.at[j], recv_sem=precv_sem.at[j],
-            device_id=(gx, lax.rem(gy + j, ny)), device_id_type=MESH,
-        )
-
-    def part_arrival(j):
-        at = lax.rem(gy + ny - j, ny)
-        return pltpu.make_async_remote_copy(
-            src_ref=part.at[at], dst_ref=part.at[at], send_sem=psend_sem.at[j], recv_sem=precv_sem.at[j],
-            device_id=(gx, lax.rem(gy + j, ny)), device_id_type=MESH,
-        )
-
-    def gather_copy(j):
-        return pltpu.make_async_remote_copy(
-            src_ref=gather.at[gx], dst_ref=gather.at[gx], send_sem=gsend_sem.at[j], recv_sem=grecv_sem.at[j],
-            device_id=(lax.rem(gx + j, nx), gy), device_id_type=MESH,
-        )
-
-    def gather_arrival(j):
-        at = lax.rem(gx + nx - j, nx)
-        return pltpu.make_async_remote_copy(
-            src_ref=gather.at[at], dst_ref=gather.at[at], send_sem=gsend_sem.at[j], recv_sem=grecv_sem.at[j],
-            device_id=(lax.rem(gx + j, nx), gy), device_id_type=MESH,
-        )
-
-    for j in range(1, ny):
-        part_copy(j).start()
-
-    def pass_on():
-        for j in range(1, ny):
-            part_arrival(j).wait_recv()
-        for y in range(ny):
-            for f in range(2):
-                gather[gx, f, y * half : (y + 1) * half, :] = part[y, f * half : (f + 1) * half, :]
-        for j in range(1, nx):
-            gather_copy(j).start()
+            k_here, cz_before = k_after, cz_here
 
     def sweep(k, buf, write, sent=None):
         @pl.loop(0, steps)
@@ -305,7 +234,7 @@
                         + get(cy, p - 1, c, at, -1) * get(buf, p, c, at, -1)
                     )
                 ) + (cz_here * next_col(here, after) + prev_col(q_before, q_here))
-                write(p, order, c, at, flat, here, get(wgt, p - 1, c, flat) * total)
+                write(p, order, c, at, flat, here, total)
                 here, q_before = after, q_here
 
             if k == 3:
@@ -313,8 +242,74 @@
                 def _():
                     store_planes(i - inner - 2, 4)
 
-    def write_second(p, order, c, at, flat, here, term):
-        second = (1.0 + (1.0 - damping)) * here + term
+    def write_first(p, order, c, at, flat, here, total):
+        twice_diag = get(wgt, p - 1, c, flat)
+        resid = get(src, p - 1, c, flat) - 0.5 * (twice_diag * here - total)
+        weight = damping / twice_diag
+        first = (2.0 * weight) * resid
+        put(wgt, p - 1, c, flat, weight)
+        put(corr1, p, c, at, first)
+        pack(2, order, c, first)
+        add_part(0, c, resid)
+
+    wait_load(2)
+    sweep(1, prev, write_first, 2)
+    start_all(plane_copies(2))
+    start_all(row_copies(2, 1))
+
+    lines = 2 * half * chunks
+    sums = jnp.sum(acc[...], axis=1)
+    per_chunk = LANES // F
+    lane_row = lax.broadcasted_iota(jnp.int32, (LANES, LANES), 0)
+    lane_col = lax.broadcasted_iota(jnp.int32, (LANES, LANES), 1)
+    pool = jnp.where(lax.rem(lane_col, per_chunk) == lax.div(lane_row, F), 1.0, 0.0)
+    pooled = jnp.dot(sums, pool, precision=HI, preferred_element_type=jnp.float32)
+    line_row = lax.broadcasted_iota(jnp.int32, (lines, LANES), 0)
+    line_col = lax.broadcasted_iota(jnp.int32, (lines, LANES), 1)
+    pooled = jnp.where(lax.div(line_col, per_chunk) == lax.rem(line_row, chunks), pooled, 0.0)
+    small = jnp.sum(pooled.reshape(2 * half, chunks, LANES), axis=1) * (1.0 / (F * F * F))
+    part[gy, 0 : 2 * half, :] = small
+
+    def part_copy(j):
+        return pltpu.make_async_remote_copy(
+            src_ref=part.at[gy], dst_ref=part.at[gy], send_sem=psend_sem.at[j], recv_sem=precv_sem.at[j],
+            device_id=(gx, lax.rem(gy + j, ny)), device_id_type=MESH,
+        )
+
+    def part_arrival(j):
+        at = lax.rem(gy + ny - j, ny)
+        return pltpu.make_async_remote_copy(
+            src_ref=part.at[at], dst_ref=part.at[at], send_sem=psend_sem.at[j], recv_sem=precv_sem.at[j],
+            device_id=(gx, lax.rem(gy + j, ny)), device_id_type=MESH,
+        )
+
+    def gather_copy(j):
+        return pltpu.make_async_remote_copy(
+            src_ref=gather.at[gx], dst_ref=gather.at[gx], send_sem=gsend_sem.at[j], recv_sem=grecv_sem.at[j],
+            device_id=(lax.rem(gx + j, nx), gy), device_id_type=MESH,
+        )
+
+    def gather_arrival(j):
+        at = lax.rem(gx + nx - j, nx)
+        return pltpu.make_async_remote_copy(
+            src_ref=gather.at[at], dst_ref=gather.at[at], send_sem=gsend_sem.at[j], recv_sem=grecv_sem.at[j],
+            device_id=(lax.rem(gx + j, nx), gy), device_id_type=MESH,
+        )
+
+    for j in range(1, ny):
+        part_copy(j).start()
+
+    def pass_on():
+        for j in range(1, ny):
+            part_arrival(j).wait_recv()
+        for y in range(ny):
+            for f in range(2):
+                gather[gx, f, y * half : (y + 1) * half, :] = part[y, f * half : (f + 1) * half, :]
+        for j in range(1, nx):
+            gather_copy(j).start()
+
+    def write_second(p, order, c, at, flat, here, total):
+        second = (1.0 + (1.0 - damping)) * here + get(wgt, p - 1, c, flat) * total
         put(corr2, p, c, at, second)
         pack(3, order, c, second)
 
@@ -379,7 +374,8 @@
         for c in range(chunks):
             out_copy(c, start, count).start()
 
-    def write_third(p, order, c, at, flat, here, term):
+    def write_third(p, order, c, at, flat, here, total):
+        term = get(wgt, p - 1, c, flat) * total
         put(src, p - 1, c, flat, ((1.0 - damping) * here + get(corr1, p, c, at)) + term)
 
     sweep(3, corr2, write_third)
@@ -463,7 +459,7 @@
             pltpu.SemaphoreType.DMA((nx,)),
         ],
         compiler_params=pltpu.CompilerParams(
-            collective_id=0, has_side_effects=True, vmem_limit_bytes=60 * 1024 * 1024
+            collective_id=0, has_side_effects=True, vmem_limit_bytes=58 * 1024 * 1024
         ),
         name="correction_main",
     )(previous, source, conductivity)

time: 55.5 us -> 56.2 us (1.013)
  Pallas kernels: 55.2 us -> 56 us
    pallas_call x1, Pallas kernels: 50.2 us -> 50.9 us  [per_device(): pl.pallas_call(functools.partial(main_kernel, nx, ny, planes, rows, chunk...]
where the time goes in v2:
time: 56.2 us; the launch traced here: 56 us
  Pallas kernels  56 us (100%)
    pallas_call x1, Pallas kernels, per_device(): pl.pallas_call(functools.partial(main_kernel, nx, ny, planes, rows, chunk...  50.9 us
    pallas_call x1, Pallas kernels, per_device(): pl.pallas_call(functools.partial(add_kernel, step_planes, rows), out_shap...  5.07 us

profile of v2, /device:TPU:0, one launch (start us, length us, event | category | flops | bytes accessed | tf_op | source)
XLA Modules:
  0.0 56.0 jit_solution(7719836921989539468)
XLA Ops:
  0.0 50.9 %correction_main.1 = (f32[16,32,2048]{2,1,0:T(8,128)}, f32[24,2048]{1,0:T(8,128)}) custom-call(f32[16,32,2048]{2,1,0:T(8,128)} %prev_hbm.1, f32[16,32,2048]{2,1,0:T(8,128)} %src_hbm.1, f32[16,32,2048]{2,1,0:T(8,128)} %cond_hbm.1), custom_call_target="tpu_custom_call" | custom-call | tf_op jit(solution)/shard_map/correction_main/pallas_call | solution.py:433
  50.9 5.1 %interpolate_add.1 = f32[16,32,2048]{2,1,0:T(8,128)} custom-call(f32[16,32,2048]{2,1,0:T(8,128)} %get-tuple-element.7.fine_ref, f32[24,2048]{1,0:T(8,128)} %get-tuple-element.8.cols_ref), custom_call_target="tpu_custom_call" | custom-call | tf_op jit(solution)/shard_map/interpolate_add/pallas_call | solution.py:467

commit v3 on v2

--- a/solution.py
+++ b/solution.py
@@ -186,6 +186,7 @@
         def cond_at(c):
             return get(cond, p, c % chunks, at)
 
+        ready = []
         k_here = cond_at(chunks - 1)
         k_after = cond_at(0)
         cz_before = k_here + next_col(k_here, k_after)
@@ -198,17 +199,21 @@
             cx_low = k_here + get(cond, p - 1, c, at)
             cy_high = k_here + get(cond, p, c, at, 1)
             cy_low = k_here + get(cond, p, c, at, -1)
-            put(cz, p - 1, c, flat, cz_here)
-            put(cx, p, c, flat, cx_high)
-            put(cx, p - 1, c, flat, cx_low)
-            put(cy, p - 1, c, at, cy_high)
-            cy[p - 1, c, pl.ds(at[0] - 1, 1), :] = cy_low[0:1]
             twice_diag = (((cx_high + cx_low) + (cy_high + cy_low)) + (cz_here + cz_low)) + 2 * reaction
-            put(wgt, p - 1, c, flat, twice_diag)
-            add_part(1, c, k_here)
+            ready.append((c, cz_here, cx_high, cx_low, cy_high, cy_low[0:1], twice_diag, k_here))
             k_here, cz_before = k_after, cz_here
-
-    def sweep(k, buf, write, sent=None):
+            if len(ready) == 4:
+                for d, c_z, c_xh, c_xl, c_yh, c_yl, twice, kept in ready:
+                    put(cz, p - 1, d, flat, c_z)
+                    put(cx, p, d, flat, c_xh)
+                    put(cx, p - 1, d, flat, c_xl)
+                    put(cy, p - 1, d, at, c_yh)
+                    cy[p - 1, d, pl.ds(at[0] - 1, 1), :] = c_yl
+                    put(wgt, p - 1, d, flat, twice)
+                    add_part(1, d, kept)
+                ready = []
+
+    def sweep(k, buf, make, write, group, sent=None):
         @pl.loop(0, steps)
         def _(i):
             p, order, edge = place_of(i)
@@ -221,6 +226,7 @@
             def here_at(c):
                 return get(buf, p, c % chunks, at)
 
+            ready = []
             q_before = get(cz, p - 1, chunks - 1, flat) * here_at(chunks - 1)
             here = here_at(0)
             for c in range(chunks):
@@ -234,26 +240,32 @@
                         + get(cy, p - 1, c, at, -1) * get(buf, p, c, at, -1)
                     )
                 ) + (cz_here * next_col(here, after) + prev_col(q_before, q_here))
-                write(p, order, c, at, flat, here, total)
+                ready.append((c, make(p, c, at, flat, here, total)))
                 here, q_before = after, q_here
+                if len(ready) == group:
+                    for d, made in ready:
+                        write(p, order, d, at, flat, *made)
+                    ready = []
 
             if k == 3:
                 @pl.when((i >= inner) & (i < 2 * inner) & (lax.rem(i - inner, 4) == 3))
                 def _():
                     store_planes(i - inner - 2, 4)
 
-    def write_first(p, order, c, at, flat, here, total):
+    def make_first(p, c, at, flat, here, total):
         twice_diag = get(wgt, p - 1, c, flat)
         resid = get(src, p - 1, c, flat) - 0.5 * (twice_diag * here - total)
         weight = damping / twice_diag
-        first = (2.0 * weight) * resid
+        return weight, (2.0 * weight) * resid, resid
+
+    def write_first(p, order, c, at, flat, weight, first, resid):
         put(wgt, p - 1, c, flat, weight)
         put(corr1, p, c, at, first)
         pack(2, order, c, first)
         add_part(0, c, resid)
 
     wait_load(2)
-    sweep(1, prev, write_first, 2)
+    sweep(1, prev, make_first, write_first, 4, 2)
     start_all(plane_copies(2))
     start_all(row_copies(2, 1))
 
@@ -308,12 +320,14 @@
         for j in range(1, nx):
             gather_copy(j).start()
 
-    def write_second(p, order, c, at, flat, here, total):
-        second = (1.0 + (1.0 - damping)) * here + get(wgt, p - 1, c, flat) * total
+    def make_second(p, c, at, flat, here, total):
+        return ((1.0 + (1.0 - damping)) * here + get(wgt, p - 1, c, flat) * total,)
+
+    def write_second(p, order, c, at, flat, second):
         put(corr2, p, c, at, second)
         pack(3, order, c, second)
 
-    sweep(2, corr1, write_second, 3)
+    sweep(2, corr1, make_second, write_second, 8, 3)
     start_all(plane_copies(3))
     start_all(row_copies(3, 1))
 
@@ -374,11 +388,14 @@
         for c in range(chunks):
             out_copy(c, start, count).start()
 
-    def write_third(p, order, c, at, flat, here, total):
+    def make_third(p, c, at, flat, here, total):
         term = get(wgt, p - 1, c, flat) * total
-        put(src, p - 1, c, flat, ((1.0 - damping) * here + get(corr1, p, c, at)) + term)
-
-    sweep(3, corr2, write_third)
+        return (((1.0 - damping) * here + get(corr1, p, c, at)) + term,)
+
+    def write_third(p, order, c, at, flat, third):
+        put(src, p - 1, c, flat, third)
+
+    sweep(3, corr2, make_third, write_third, 8)
     store_planes(planes - 3, 3)
     store_planes(0, 1)
 

time: 56.2 us -> 55.5 us (0.988)
  Pallas kernels: 56 us -> 55.3 us
    pallas_call x1, Pallas kernels: 50.9 us -> 50.2 us  [per_device(): pl.pallas_call(functools.partial(main_kernel, nx, ny, planes, rows, chunk...]
where the time goes in v3:
time: 55.5 us; the launch traced here: 55.3 us
  Pallas kernels  55.3 us (100%)
    pallas_call x1, Pallas kernels, per_device(): pl.pallas_call(functools.partial(main_kernel, nx, ny, planes, rows, chunk...  50.2 us
    pallas_call x1, Pallas kernels, per_device(): pl.pallas_call(functools.partial(add_kernel, step_planes, rows), out_shap...  5.07 us

profile of v3, /device:TPU:0, one launch (start us, length us, event | category | flops | bytes accessed | tf_op | source)
XLA Modules:
  0.0 55.3 jit_solution(2271502362749546288)
XLA Ops:
  0.0 50.2 %correction_main.1 = (f32[16,32,2048]{2,1,0:T(8,128)}, f32[24,2048]{1,0:T(8,128)}) custom-call(f32[16,32,2048]{2,1,0:T(8,128)} %prev_hbm.1, f32[16,32,2048]{2,1,0:T(8,128)} %src_hbm.1, f32[16,32,2048]{2,1,0:T(8,128)} %cond_hbm.1), custom_call_target="tpu_custom_call" | custom-call | tf_op jit(solution)/shard_map/correction_main/pallas_call | solution.py:450
  50.2 5.1 %interpolate_add.1 = f32[16,32,2048]{2,1,0:T(8,128)} custom-call(f32[16,32,2048]{2,1,0:T(8,128)} %get-tuple-element.7.fine_ref, f32[24,2048]{1,0:T(8,128)} %get-tuple-element.8.cols_ref), custom_call_target="tpu_custom_call" | custom-call | tf_op jit(solution)/shard_map/interpolate_add/pallas_call | solution.py:484

commit v4 on v3

--- a/solution.py
+++ b/solution.py
@@ -38,7 +38,7 @@
     nx, ny, planes, rows, chunks,
     prev_hbm, src_hbm, cond_hbm, out_hbm, cols_ref,
     cond, prev, corr1, corr2, src, wgt, cx, cy, cz,
-    row_send, row_recv, acc, part, gather, coarse,
+    acc, part, gather, coarse,
     load_sem, out_sem, send_sem, recv_sem, psend_sem, precv_sem, gsend_sem, grecv_sem,
 ):
     gx, gy = lax.axis_index("gx"), lax.axis_index("gy")
@@ -100,15 +100,19 @@
             remote(buf.at[planes, :, body_rows, :], buf.at[0, :, body_rows, :], 2 * k + 1, x_next),
         )
 
-    cut = inner * chunks
-
     def row_copies(k, late):
-        lines = pl.ds(cut, 2 * chunks) if late else pl.ds(0, cut)
-        sem = 16 + 4 * k + 2 * late
-        return (
-            remote(row_send.at[k, 0, lines], row_recv.at[k, 0, lines], sem, y_prev),
-            remote(row_send.at[k, 1, lines], row_recv.at[k, 1, lines], sem + 1, y_next),
-        )
+        buf, copies = fields[k], []
+        groups = ((1, 1), (planes, 1)) if late else ((2, inner),)
+        for g, (first, count) in enumerate(groups):
+            sem = 8 + 6 * k + (2 + 2 * g if late else 0)
+            span = pl.ds(first, count)
+
+            def row(at):
+                return buf.at[span, :, pl.ds(at, 1), :]
+
+            copies.append(remote(row(TOP), row(last_row + 1), sem, y_prev))
+            copies.append(remote(row(last_row), row(TOP - 1), sem + 1, y_next))
+        return tuple(copies)
 
     def start_all(copies):
         for copy in copies:
@@ -117,40 +121,12 @@
     def wait_recv(copies):
         for copy in copies:
             copy.wait_recv()
-
-    def pack(k, order, c, block):
-        at = order * chunks + c
-        row_send[k, 0, pl.ds(at, 1), :] = block[0:1]
-        row_send[k, 1, pl.ds(at, 1), :] = block[15:16]
-
-    def pack_all(k):
-        buf = fields[k]
-
-        @pl.loop(0, planes)
-        def _(order):
-            p = lax.rem(order + 1, planes) + 1
-            for c in range(chunks):
-                at = order * chunks + c
-                row_send[k, 0, pl.ds(at, 1), :] = buf[p, c, TOP : TOP + 1, :]
-                row_send[k, 1, pl.ds(at, 1), :] = buf[p, c, last_row : last_row + 1, :]
-
-    def unpack(k, first, last):
-        buf = fields[k]
-
-        @pl.loop(first, last)
-        def _(order):
-            p = lax.rem(order + 1, planes) + 1
-            for c in range(chunks):
-                at = order * chunks + c
-                buf[p, c, last_row + 1 : last_row + 2, :] = row_recv[k, 0, pl.ds(at, 1), :]
-                buf[p, c, TOP - 1 : TOP, :] = row_recv[k, 1, pl.ds(at, 1), :]
 
     def arrivals(i, ks, sent=None):
         @pl.when(i == inner)
         def _():
             for k in ks:
                 wait_recv(row_copies(k, 0))
-                unpack(k, 0, inner)
 
         @pl.when(i == 2 * inner)
         def _():
@@ -158,13 +134,11 @@
                 start_all(row_copies(sent, 0))
             for k in ks:
                 wait_recv(row_copies(k, 1))
-                unpack(k, inner, planes)
                 wait_recv(plane_copies(k))
 
     for k in (0, 1):
         wait_load(k)
         start_all(plane_copies(k))
-        pack_all(k)
         start_all(row_copies(k, 0))
         start_all(row_copies(k, 1))
     acc[...] = jnp.zeros_like(acc)
@@ -261,7 +235,6 @@
     def write_first(p, order, c, at, flat, weight, first, resid):
         put(wgt, p - 1, c, flat, weight)
         put(corr1, p, c, at, first)
-        pack(2, order, c, first)
         add_part(0, c, resid)
 
     wait_load(2)
@@ -325,7 +298,6 @@
 
     def write_second(p, order, c, at, flat, second):
         put(corr2, p, c, at, second)
-        pack(3, order, c, second)
 
     sweep(2, corr1, make_second, write_second, 8, 3)
     start_all(plane_copies(3))
@@ -460,8 +432,6 @@
             pltpu.VMEM((planes + 1, chunks, rows, LANES), f32),
             pltpu.VMEM((planes, chunks, rows + 8, LANES), f32),
             plain,
-            pltpu.VMEM((4, 2, planes * chunks, LANES), f32),
-            pltpu.VMEM((4, 2, planes * chunks, LANES), f32),
             pltpu.VMEM((2 * half * chunks, 8, LANES), f32),
             pltpu.VMEM((ny, 8, LANES), f32),
             pltpu.VMEM((nx, 2, ny * half, LANES), f32),

time: 55.5 us -> 54.9 us (0.989)
  Pallas kernels: 55.3 us -> 54.7 us
    pallas_call x1, Pallas kernels: 50.2 us -> 49.6 us  [per_device(): pl.pallas_call(functools.partial(main_kernel, nx, ny, planes, rows, chunk...]
where the time goes in v4:
time: 54.9 us; the launch traced here: 54.7 us
  Pallas kernels  54.7 us (100%)
    pallas_call x1, Pallas kernels, per_device(): pl.pallas_call(functools.partial(main_kernel, nx, ny, planes, rows, chunk...  49.6 us
    pallas_call x1, Pallas kernels, per_device(): pl.pallas_call(functools.partial(add_kernel, step_planes, rows), out_shap...  5.07 us

profile of v4, /device:TPU:0, one launch (start us, length us, event | category | flops | bytes accessed | tf_op | source)
XLA Modules:
  0.0 54.7 jit_solution(4145855237715179431)
XLA Ops:
  0.0 49.6 %correction_main.1 = (f32[16,32,2048]{2,1,0:T(8,128)}, f32[24,2048]{1,0:T(8,128)}) custom-call(f32[16,32,2048]{2,1,0:T(8,128)} %prev_hbm.1, f32[16,32,2048]{2,1,0:T(8,128)} %src_hbm.1, f32[16,32,2048]{2,1,0:T(8,128)} %cond_hbm.1), custom_call_target="tpu_custom_call" | custom-call | tf_op jit(solution)/shard_map/correction_main/pallas_call | solution.py:422
  49.7 5.1 %interpolate_add.1 = f32[16,32,2048]{2,1,0:T(8,128)} custom-call(f32[16,32,2048]{2,1,0:T(8,128)} %get-tuple-element.7.fine_ref, f32[24,2048]{1,0:T(8,128)} %get-tuple-element.8.cols_ref), custom_call_target="tpu_custom_call" | custom-call | tf_op jit(solution)/shard_map/interpolate_add/pallas_call | solution.py:454

commit v5 on v4

--- a/solution.py
+++ b/solution.py
@@ -36,9 +36,9 @@
 
 def main_kernel(
     nx, ny, planes, rows, chunks,
-    prev_hbm, src_hbm, cond_hbm, out_hbm, cols_ref,
+    prev_hbm, src_hbm, cond_hbm, out_hbm,
     cond, prev, corr1, corr2, src, wgt, cx, cy, cz,
-    acc, part, gather, coarse,
+    acc, part, gather, coarse, across,
     load_sem, out_sem, send_sem, recv_sem, psend_sem, precv_sem, gsend_sem, grecv_sem,
 ):
     gx, gy = lax.axis_index("gx"), lax.axis_index("gy")
@@ -338,6 +338,15 @@
         block.append(pltpu.roll(plane, turn, 0)[0:8])
     block = jnp.concatenate(block, axis=0)
     ccols = chunks * LANES // F
+    row = lax.broadcasted_iota(jnp.int32, (rows, LANES), 0)
+    row_base = lax.div(row, F) + 1
+    row_offset = (lax.rem(row, F).astype(jnp.float32) + 0.5) / F - 0.5
+    row_side = jnp.where(row_offset > 0, row_base + 1, row_base - 1)
+    row_weights = [
+        jnp.where(row_base == b, 1.0 - jnp.abs(row_offset), 0.0)
+        + jnp.where(row_side == b, jnp.abs(row_offset), 0.0)
+        for b in range(half + 2)
+    ]
     for c in range(chunks):
         fine = c * LANES + lane_col
         base = lax.div(fine, F)
@@ -345,9 +354,12 @@
         side = lax.rem(jnp.where(offset > 0, base + 1, base + ccols - 1), ccols)
         spread = jnp.where(lane_row == base, 1.0 - jnp.abs(offset), 0.0)
         spread = spread + jnp.where(lane_row == side, jnp.abs(offset), 0.0)
-        cols_ref[:, c * LANES : (c + 1) * LANES] = jnp.dot(
-            block, spread, precision=HI, preferred_element_type=jnp.float32
-        )
+        along = jnp.dot(block, spread, precision=HI, preferred_element_type=jnp.float32)
+        for a in range(3):
+            total = row_weights[0] * along[8 * a : 8 * a + 1]
+            for b in range(1, half + 2):
+                total = total + row_weights[b] * along[8 * a + b : 8 * a + b + 1]
+            across[a, c] = total
 
     def out_copy(c, start, count):
         return pltpu.make_async_copy(
@@ -362,7 +374,10 @@
 
     def make_third(p, c, at, flat, here, total):
         term = get(wgt, p - 1, c, flat) * total
-        return (((1.0 - damping) * here + get(corr1, p, c, at)) + term,)
+        side = 2 * lax.div(p - 1, F // 2)
+        weight = jnp.abs(((p - 1).astype(jnp.float32) + 0.5) / F - 0.5)
+        inter = (1.0 - weight) * get(across, 1, c, flat) + weight * get(across, side, c, flat)
+        return ((((1.0 - damping) * here + get(corr1, p, c, at)) + term) + inter,)
 
     def write_third(p, order, c, at, flat, third):
         put(src, p - 1, c, flat, third)
@@ -381,36 +396,6 @@
     pltpu.make_async_copy(src, src, out_sem).wait()
 
 
-def add_kernel(step_planes, rows, fine_ref, cols_ref, out_ref, across):
-    step = pl.program_id(0)
-    half = rows // F
-
-    @pl.when(step == 0)
-    def _():
-        row = lax.broadcasted_iota(jnp.int32, (rows, LANES), 0)
-        base = lax.div(row, F) + 1
-        offset = (lax.rem(row, F).astype(jnp.float32) + 0.5) / F - 0.5
-        side = jnp.where(offset > 0, base + 1, base - 1)
-        weights = [
-            jnp.where(base == b, 1.0 - jnp.abs(offset), 0.0) + jnp.where(side == b, jnp.abs(offset), 0.0)
-            for b in range(half + 2)
-        ]
-        for a in range(3):
-            for c in range(cols_ref.shape[1] // LANES):
-                at = pl.ds(c * LANES, LANES)
-                total = weights[0] * cols_ref[8 * a : 8 * a + 1, at]
-                for b in range(1, half + 2):
-                    total = total + weights[b] * cols_ref[8 * a + b : 8 * a + b + 1, at]
-                across[a, :, at] = total
-
-    for q in range(step_planes):
-        plane = step * step_planes + q
-        offset = (plane.astype(jnp.float32) + 0.5) / F - 0.5
-        side = jnp.where(offset > 0, 2, 0)
-        weight = jnp.abs(offset)
-        out_ref[q] = fine_ref[q] + ((1.0 - weight) * across[1] + weight * across[side])
-
-
 def per_device(nx, ny, previous, source, conductivity):
     planes, rows, cols = previous.shape
     chunks = cols // LANES
@@ -419,14 +404,11 @@
     padded = pltpu.VMEM((planes + 2, chunks, rows + 16, LANES), f32)
     plain = pltpu.VMEM((planes, chunks, rows, LANES), f32)
     any_spec = pl.BlockSpec(memory_space=pl.ANY)
-    fine, along = pl.pallas_call(
+    return pl.pallas_call(
         functools.partial(main_kernel, nx, ny, planes, rows, chunks),
-        out_shape=(
-            jax.ShapeDtypeStruct((planes, rows, cols), f32),
-            jax.ShapeDtypeStruct((24, cols), f32),
-        ),
+        out_shape=jax.ShapeDtypeStruct((planes, rows, cols), f32),
         in_specs=[any_spec] * 3,
-        out_specs=(any_spec, pl.BlockSpec(memory_space=pltpu.VMEM)),
+        out_specs=any_spec,
         scratch_shapes=[
             padded, padded, padded, padded, plain, plain,
             pltpu.VMEM((planes + 1, chunks, rows, LANES), f32),
@@ -436,6 +418,7 @@
             pltpu.VMEM((ny, 8, LANES), f32),
             pltpu.VMEM((nx, 2, ny * half, LANES), f32),
             pltpu.VMEM((nx, ny * half, LANES), f32),
+            pltpu.VMEM((3, chunks, rows, LANES), f32),
             pltpu.SemaphoreType.DMA((3,)),
             pltpu.SemaphoreType.DMA,
             pltpu.SemaphoreType.DMA((32,)),
@@ -450,20 +433,6 @@
         ),
         name="correction_main",
     )(previous, source, conductivity)
-    step_planes = 4
-    return pl.pallas_call(
-        functools.partial(add_kernel, step_planes, rows),
-        out_shape=jax.ShapeDtypeStruct((planes, rows, cols), f32),
-        grid=(planes // step_planes,),
-        in_specs=[
-            pl.BlockSpec((step_planes, rows, cols), lambda i: (i, 0, 0)),
-            pl.BlockSpec((24, cols), lambda i: (0, 0)),
-        ],
-        out_specs=pl.BlockSpec((step_planes, rows, cols), lambda i: (i, 0, 0)),
-        scratch_shapes=[pltpu.VMEM((3, rows, cols), f32)],
-        compiler_params=pltpu.CompilerParams(vmem_limit_bytes=60 * 1024 * 1024),
-        name="interpolate_add",
-    )(fine, along)
 
 
 def solution(mesh):

time: 54.9 us -> 54.6 us (level)
  Pallas kernels: 54.7 us -> 49.7 us
  local copies, waits for them, and re-layouts: 0 us -> 4.7 us
    pallas_call x1 -> x0, Pallas kernels: 5.07 us -> none  [per_device(): pl.pallas_call(functools.partial(add_kernel, step_planes, rows), out_shap...]
    unnamed x0 -> x1, local copies, waits for them, and re-layouts: none -> 4.7 us
where the time goes in v5:
time: 54.6 us; the launch traced here: 54.4 us
  Pallas kernels  49.7 us (91%)
  local copies, waits for them, and re-layouts  4.7 us (9%)
    pallas_call x1, Pallas kernels, per_device(): pl.pallas_call(functools.partial(main_kernel, nx, ny, planes, rows, chunk...  49.7 us
    unnamed x1, local copies, waits for them, and re-layouts  4.7 us

profile of v5, /device:TPU:0, one launch (start us, length us, event | category | flops | bytes accessed | tf_op | source)
XLA Modules:
  0.0 54.4 jit_solution(1837404751435899817)
XLA Ops:
  0.0 49.7 %correction_main.1 = f32[16,32,2048]{2,1,0:T(8,128)} custom-call(f32[16,32,2048]{2,1,0:T(8,128)} %prev_hbm.1, f32[16,32,2048]{2,1,0:T(8,128)} %src_hbm.1, f32[16,32,2048]{2,1,0:T(8,128)} %cond_hbm.1), custom_call_target="tpu_custom_call" | custom-call | tf_op jit(solution)/shard_map/correction_main/pallas_call | solution.py:407
  49.7 4.7 %copy.5 = f32[16,32,2048]{2,1,0:T(8,128)} copy(f32[16,32,2048]{2,1,0:T(8,128)} %correction_main.1) | data formatting | bytes 8388608

commit v6 on v1

--- a/solution.py
+++ b/solution.py
@@ -38,7 +38,7 @@
     nx, ny, planes, rows, chunks,
     prev_hbm, src_hbm, cond_hbm, out_hbm, cols_ref,
     cond, prev, corr1, corr2, src, wgt, cx, cy, cz,
-    row_send, row_recv, acc, part, gather, coarse,
+    acc, part, gather, coarse,
     load_sem, out_sem, send_sem, recv_sem, psend_sem, precv_sem, gsend_sem, grecv_sem,
 ):
     gx, gy = lax.axis_index("gx"), lax.axis_index("gy")
@@ -100,15 +100,19 @@
             remote(buf.at[planes, :, body_rows, :], buf.at[0, :, body_rows, :], 2 * k + 1, x_next),
         )
 
-    cut = inner * chunks
-
     def row_copies(k, late):
-        lines = pl.ds(cut, 2 * chunks) if late else pl.ds(0, cut)
-        sem = 16 + 4 * k + 2 * late
-        return (
-            remote(row_send.at[k, 0, lines], row_recv.at[k, 0, lines], sem, y_prev),
-            remote(row_send.at[k, 1, lines], row_recv.at[k, 1, lines], sem + 1, y_next),
-        )
+        buf, copies = fields[k], []
+        groups = ((1, 1), (planes, 1)) if late else ((2, inner),)
+        for g, (first, count) in enumerate(groups):
+            sem = 8 + 6 * k + (2 + 2 * g if late else 0)
+            span = pl.ds(first, count)
+
+            def row(at):
+                return buf.at[span, :, pl.ds(at, 1), :]
+
+            copies.append(remote(row(TOP), row(last_row + 1), sem, y_prev))
+            copies.append(remote(row(last_row), row(TOP - 1), sem + 1, y_next))
+        return tuple(copies)
 
     def start_all(copies):
         for copy in copies:
@@ -117,40 +121,12 @@
     def wait_recv(copies):
         for copy in copies:
             copy.wait_recv()
-
-    def pack(k, order, c, block):
-        at = order * chunks + c
-        row_send[k, 0, pl.ds(at, 1), :] = block[0:1]
-        row_send[k, 1, pl.ds(at, 1), :] = block[15:16]
-
-    def pack_all(k):
-        buf = fields[k]
-
-        @pl.loop(0, planes)
-        def _(order):
-            p = lax.rem(order + 1, planes) + 1
-            for c in range(chunks):
-                at = order * chunks + c
-                row_send[k, 0, pl.ds(at, 1), :] = buf[p, c, TOP : TOP + 1, :]
-                row_send[k, 1, pl.ds(at, 1), :] = buf[p, c, last_row : last_row + 1, :]
-
-    def unpack(k, first, last):
-        buf = fields[k]
-
-        @pl.loop(first, last)
-        def _(order):
-            p = lax.rem(order + 1, planes) + 1
-            for c in range(chunks):
-                at = order * chunks + c
-                buf[p, c, last_row + 1 : last_row + 2, :] = row_recv[k, 0, pl.ds(at, 1), :]
-                buf[p, c, TOP - 1 : TOP, :] = row_recv[k, 1, pl.ds(at, 1), :]
 
     def arrivals(i, ks, sent=None):
         @pl.when(i == inner)
         def _():
             for k in ks:
                 wait_recv(row_copies(k, 0))
-                unpack(k, 0, inner)
 
         @pl.when(i == 2 * inner)
         def _():
@@ -158,13 +134,11 @@
                 start_all(row_copies(sent, 0))
             for k in ks:
                 wait_recv(row_copies(k, 1))
-                unpack(k, inner, planes)
                 wait_recv(plane_copies(k))
 
     for k in (0, 1):
         wait_load(k)
         start_all(plane_copies(k))
-        pack_all(k)
         start_all(row_copies(k, 0))
         start_all(row_copies(k, 1))
     acc[...] = jnp.zeros_like(acc)
@@ -220,7 +194,6 @@
             first = (2.0 * weight) * resid
             put(wgt, p - 1, c, flat, weight)
             put(corr1, p, c, at, first)
-            pack(2, order, c, first)
             add_part(0, c, resid)
             add_part(1, c, k_here)
             k_here, v_here, cz_before, q_before = k_after, v_after, cz_here, q_here
@@ -316,7 +289,6 @@
     def write_second(p, order, c, at, flat, here, term):
         second = (1.0 + (1.0 - damping)) * here + term
         put(corr2, p, c, at, second)
-        pack(3, order, c, second)
 
     sweep(2, corr1, write_second, 3)
     start_all(plane_copies(3))
@@ -447,8 +419,6 @@
             pltpu.VMEM((planes + 1, chunks, rows, LANES), f32),
             pltpu.VMEM((planes, chunks, rows + 8, LANES), f32),
             plain,
-            pltpu.VMEM((4, 2, planes * chunks, LANES), f32),
-            pltpu.VMEM((4, 2, planes * chunks, LANES), f32),
             pltpu.VMEM((2 * half * chunks, 8, LANES), f32),
             pltpu.VMEM((ny, 8, LANES), f32),
             pltpu.VMEM((nx, 2, ny * half, LANES), f32),

time: 55.5 us -> 55 us (level)
  no operation moved by 1% of the time
where the time goes in v6:
time: 55 us; the launch traced here: 54.8 us
  Pallas kernels  54.8 us (100%)
    pallas_call x1, Pallas kernels, per_device(): pl.pallas_call(functools.partial(main_kernel, nx, ny, planes, rows, chunk...  49.8 us
    pallas_call x1, Pallas kernels, per_device(): pl.pallas_call(functools.partial(add_kernel, step_planes, rows), out_shap...  5.07 us

profile of v6, /device:TPU:0, one launch (start us, length us, event | category | flops | bytes accessed | tf_op | source)
XLA Modules:
  0.0 54.8 jit_solution(15867898431892920105)
XLA Ops:
  0.0 49.8 %correction_main.1 = (f32[16,32,2048]{2,1,0:T(8,128)}, f32[24,2048]{1,0:T(8,128)}) custom-call(f32[16,32,2048]{2,1,0:T(8,128)} %prev_hbm.1, f32[16,32,2048]{2,1,0:T(8,128)} %src_hbm.1, f32[16,32,2048]{2,1,0:T(8,128)} %cond_hbm.1), custom_call_target="tpu_custom_call" | custom-call | tf_op jit(solution)/shard_map/correction_main/pallas_call | solution.py:409
  49.8 5.1 %interpolate_add.1 = f32[16,32,2048]{2,1,0:T(8,128)} custom-call(f32[16,32,2048]{2,1,0:T(8,128)} %get-tuple-element.7.fine_ref, f32[24,2048]{1,0:T(8,128)} %get-tuple-element.8.cols_ref), custom_call_target="tpu_custom_call" | custom-call | tf_op jit(solution)/shard_map/interpolate_add/pallas_call | solution.py:441
